TPU v7x, 32 devices: a whole 2x2x4 slice. The times are simulated.
32 devices in a mesh: tm: 4 (over z), space: 8 (over y, x, core).
Axes of the slice: x: 2, y: 2, z: 4, core: 2. Of those that a mesh axis runs over, the one named last changes fastest.
Arguments:
- snaps: bfloat16 [4096, 3, 16384], P('tm', None, 'space')
- phase_bin: int32 [4096], P('tm'), may hold values from 0 to 15, as said below
- owner_order: int32 [16], replicated, may hold values from 0 to 15, each once
- modes: bfloat16 [16, 128, 3, 16384], P(None, None, None, 'space'), may hold values from -0.02734375 to 0.02734375
Outputs:
- phase_mean: bfloat16 [16, 3, 16384], P('tm', None, 'space')
- coefficients: float32 [4096, 128], P('tm')
Inputs may be any that keep to these rules, and one draw needn't show every extreme that they name: `phase_bin`: every bin is named by at least one snapshot; in each aligned block of 1024 snapshots no bin is named more than 128 times.
All inputs are finite; a program needn't handle non-finite values.
Results may differ from a plain program's by a relative error of at most 0.0068.
Values may be sent and summed in bfloat16 or wider, within the bound.
A program may use at most 192 MiB of HBM per device.

v0:
```python
import jax
import jax.numpy as jnp
from jax import lax
from jax.sharding import PartitionSpec as P


def on_device(snaps, phase_bin, owner_order, modes):
    snap_rows = snaps.shape[0]
    cell_count = snaps.shape[2]
    bin_total = modes.shape[0]
    mode_count = modes.shape[1]
    width = 3 * cell_count
    capacity = 2 * snap_rows // bin_total
    flattened = snaps.reshape(snap_rows, width)
    bin_ids = lax.broadcasted_iota(jnp.int32, (bin_total, 1), 0)
    matches = phase_bin[None, :] == bin_ids
    onehot = matches.astype(jnp.bfloat16)
    reorder = (owner_order[:, None] == bin_ids[:, 0][None, :]).astype(jnp.bfloat16)
    chosen = jnp.dot(reorder, onehot, preferred_element_type=jnp.float32)
    chosen_bf = chosen.astype(jnp.bfloat16)
    partial_sums = jnp.dot(chosen_bf, flattened, preferred_element_type=jnp.float32)
    partial_counts = jnp.sum(chosen, axis=1)
    total_sums, total_counts = lax.psum((partial_sums, partial_counts), "tm")
    all_mean = (total_sums / total_counts[:, None]).astype(jnp.bfloat16)
    own_rows = bin_total // lax.axis_size("tm")
    own_mean = lax.dynamic_slice_in_dim(all_mean, lax.axis_index("tm") * own_rows, own_rows, 0)
    phase_mean = own_mean.reshape(own_mean.shape[0], 3, cell_count)
    row_numbers = jnp.arange(bin_total, dtype=jnp.int32)
    inverse = jnp.zeros((bin_total,), jnp.int32).at[owner_order].set(row_numbers)
    mean_by_bin = jnp.take(all_mean, inverse, axis=0)
    match_int = matches.astype(jnp.int32)
    ranks = jnp.cumsum(match_int, axis=1) - 1
    slot = jnp.sum(match_int * ranks, axis=0)
    target = phase_bin * capacity + slot
    snap_numbers = jnp.arange(snap_rows, dtype=jnp.int32)
    source = jnp.full((bin_total * capacity,), snap_rows, jnp.int32).at[target].set(snap_numbers)
    gathered = jnp.take(flattened, source, axis=0, mode="fill", fill_value=0)
    gathered = gathered.reshape(bin_total, capacity, width)
    grouped = (gathered.astype(jnp.float32) - mean_by_bin.astype(jnp.float32)[:, None, :]).astype(
        jnp.bfloat16
    )
    modes_flat = modes.reshape(bin_total, mode_count, width)
    products = lax.dot_general(
        grouped, modes_flat, (((2,), (2,)), ((0,), (0,))), preferred_element_type=jnp.float32
    )
    picked = jnp.take(products.reshape(bin_total * capacity, mode_count), target, axis=0)
    coefficients = lax.psum(picked, "space")
    return (phase_mean, coefficients)


def solution(mesh):
    in_specs = (P("tm", None, "space"), P("tm"), P(), P(None, None, None, "space"))
    out_specs = (P("tm", None, "space"), P("tm", None))
    return jax.shard_map(
        on_device, mesh=mesh, in_specs=in_specs, out_specs=out_specs, check_vma=False
    )
```

profile of v0, /device:TPU:0, one launch (start us, length us, event | category | flops | bytes accessed | tf_op | source)
XLA Modules:
  0.0 239.0 jit_solution(14934051923834580583)
XLA Ops:
  7.2 0.0 copy-start
  7.2 0.0 copy-start.1
  7.2 0.0 all-reduce.3.cloned.1.call-start
  7.2 16.7 %copy.9 = bf16[1024,3,2048]{0,2,1:T(8,128)(2,1)} copy(bf16[1024,3,2048]{2,0,1:T(8,128)(2,1)} %param.4) | data formatting | bytes 25165824 | tf_op args[0]
  23.9 0.0 copy-done
  23.9 0.0 copy-done.1
  23.9 0.3 fusion.17
  24.2 8.7 %fusion.7 = f32[16,6144]{1,0:T(8,128)} fusion(bf16[1024,6144]{0,1:T(8,128)(2,1)} %bitcast.19, bf16[16,1024]{1,0:T(8,128)(2,1)S(1)} %get-tuple-element.5), kind=kOutput, calls=%fused_computation.19 | convolution fusion | flops 201326592 | bytes 13008896 | tf_op jit(solution)/shard_map/dot_general | solution.py:21
  32.9 0.0 all-reduce.3.cloned.1.call-update
  32.9 0.0 all-reduce.5.cloned.1.call-start
  33.0 16.7 %copy.12 = bf16[1024,6144]{1,0:T(8,128)(2,1)} copy(bf16[1024,6144]{0,1:T(8,128)(2,1)} %bitcast.20) | data formatting | bytes 25165824 | tf_op jit(solution)/shard_map/reshape | solution.py:14
  49.7 0.6 scatter_custom_fusion.1
  50.3 13.5 %psum.22 = f32[16]{0:T(128)S(1)} all-reduce(f32[16]{0:T(128)S(1)} %get-tuple-element.4), channel_id=1, replica_groups=mesh['tm'=4,'space'=8] {'tm'}, use_global_device_ids=true, to_apply=%region_2.0 | all-reduce | flops 16 | bytes 128 | tf_op jit(solution)/shard_map/psum | solution.py:23
  63.8 4.5 %reduce-window.6 = s32[16,8,128]{2,1,0:T(8,128)S(1)} reduce-window(s32[16,8,128]{2,1,0:T(8,128)S(1)} %fusion.5, s32[]{:T(128)} %constant.40.clone.1), window={size=1x1x128 pad=0_0x0_0x127_0}, to_apply=%region_3.0 | reduce-window | flops 2080768 | bytes 131076 | tf_op jit(solution)/shard_map/reduce-window
  68.4 0.1 slice.14
  68.4 0.1 copy.10
  68.6 0.1 copy.11
  68.7 0.1 select_reduce_fusion
  68.8 4.5 %scatter_custom_fusion = s32[2048]{0:T(1024)S(1)} fusion(s32[1024]{0:T(1024)S(1)} %get-tuple-element.3, s32[1024]{0:T(1024)S(1)} %iota.22, s32[]{:T(128)} %constant.65.clone.1), kind=kCustom, calls=%fused_computation.29 | custom fusion | bytes 8196 | tf_op jit(solution)/shard_map/scatter | solution.py:36
  73.3 32.6 %copy.13 = bf16[16,128,3,2048]{1,3,2,0:T(8,128)(2,1)} copy(bf16[16,128,3,2048]{3,1,2,0:T(8,128)(2,1)} %param.7) | data formatting | bytes 50331648 | tf_op args[3]
  106.0 48.0 %gather_fusion = bf16[2048,6144]{1,0:T(8,128)(2,1)} fusion(bf16[1024,6144]{1,0:T(8,128)(2,1)} %copy.12, s32[2048]{0:T(1024)S(1)} %fusion.10), kind=kCustom, calls=%fused_computation | custom fusion | bytes 50339840 | tf_op jit(solution)/shard_map/jit(_take)/gather | solution.py:37
  154.0 0.0 all-reduce.3.cloned.1.call-done
  154.0 1.1 divide_convert_fusion
  155.1 0.7 gather_fusion.1
  155.8 0.1 select_convert_fusion
  155.9 17.7 %fusion = f32[16,128,128]{2,1,0:T(8,128)S(1)} fusion(bf16[16,128,6144]{1,2,0:T(8,128)(2,1)} %bitcast.21, f32[16,6144]{1,0:T(8,128)S(1)} %select_convert_fusion, bf16[16,128,6144]{2,1,0:T(8,128)(2,1)} %bitcast.22, pred[16,128]{1,0:T(8,128)(4,1)S(1)} %and_bitcast_fusion), kind=kOutput, calls=%fused_computation.6 | convolution fusion | flops 3271557120 | bytes 51775488 | tf_op jit(solution)/shard_map/dot_general | solution.py:43
  173.6 2.8 %gather_fusion.2 = f32[1024,128]{1,0:T(8,128)S(1)} fusion(f32[2048,128]{1,0:T(8,128)S(1)} %bitcast.23, s32[1024]{0:T(1024)S(1)} %broadcast_clamp_fusion), kind=kCustom, calls=%fused_computation.2 | custom fusion | bytes 1052672 | tf_op jit(solution)/shard_map/jit(_take)/gather | solution.py:46
  176.4 1.0 broadcast_select_fusion
  177.4 0.0 all-reduce.5.cloned.1.call-update
  177.4 0.7 constant_dynamic-slice_fusion
  178.1 52.2 %all-reduce.5.cloned.1.call-done = f32[1024,128]{1,0:T(8,128)} async-done(((f32[1024,128]{1,0:T(8,128)}), f32[1024,128]{1,0:T(8,128)}) %all-reduce.5.cloned.1.call-update) | async-done | bytes 524304 | tf_op jit(solution)/shard_map/psum | solution.py:47
  230.3 1.9 copy.18
  (13 shorter events, 0.1 us)
Async XLA Ops:
  7.2 16.8 %copy-start = (s32[1024]{0:T(1024)S(1)}, s32[1024]{0:T(1024)}, u32[]{:S(2)}) copy-start(s32[1024]{0:T(1024)} %param.5) | copy-start | bytes 12292
  7.2 16.7 %copy-start.1 = (s32[16]{0:T(128)S(1)}, s32[16]{0:T(128)}, u32[]{:S(2)}) copy-start(s32[16]{0:T(128)} %param.6) | copy-start | bytes 196
  7.2 146.8 %all-reduce.3.cloned.1.call-start = ((), (), s32[]{:S(2)}) async-start(), calls=%async_computation | async-start | bytes 786432 | tf_op jit(solution)/shard_map/psum | solution.py:23
  32.9 197.3 %all-reduce.5.cloned.1.call-start = ((), (), s32[]{:S(2)}) async-start(), calls=%async_computation.1 | async-start | bytes 1048576 | tf_op jit(solution)/shard_map/psum | solution.py:47
Sparse Core Ops, SparseCore 0:
  33.1 39.8 all-reduce.2
  177.5 52.6 all-reduce.4
where the time goes:
time: 241 us; the launch traced here: 239 us
  local copies, waits for them, and re-layouts  125 us (52%)
  waiting for transfers between devices  52.2 us (22%)
  matrix products  26.7 us (11%)
  between operations  14.2 us (6%)
  blocking collectives  13.5 us (6%)
  other arithmetic  6.89 us (3%)
    psum x1, waiting for transfers between devices, on_device(): coefficients = lax.psum(picked, 'space')  52.2 us
    unnamed x7, local copies, waits for them, and re-layouts  51.2 us
    gather x1, local copies, waits for them, and re-layouts, on_device(): gathered = jnp.take(flattened, source, axis=0, mode='fill', fill_value=0)  48 us
    dot_general x1, matrix products, on_device(): lax.dot_general(grouped, modes_flat, (((2,), (2,)), ((0,), (0,))), prefer...  17.7 us
    reshape x1, local copies, waits for them, and re-layouts, on_device(): flattened = snaps.reshape(snap_rows, width)  16.7 us
    psum x1, blocking collectives, on_device(): total_sums, total_counts = lax.psum((partial_sums, partial_counts), 'tm')  13.5 us
    dot_general x1, matrix products, on_device(): jnp.dot(chosen_bf, flattened, preferred_element_type=jnp.float32)  8.7 us
  transfers between devices with their start and end apart: 2, of which 1 were waited for; matrix products, arithmetic and copies ran while one was open for 45% of the time, Pallas kernels for 0%

commit v1 on v0

v1 whole, which is shorter than its diff:
```python
import functools

import jax
import jax.numpy as jnp
from jax import lax
from jax.experimental import pallas as pl
from jax.experimental.pallas import tpu as pltpu
from jax.sharding import PartitionSpec as P

MESH = pl.DeviceIdType.MESH
F32 = jnp.float32
BF16 = jnp.bfloat16
NT = (((1,), (1,)), ((), ()))


def kernel(
    tm, space, binrow, binb, ownb, snaps, modes, coef_out, mean_out,
    X, mo, acc, sums, cnt, rsum, rcnt, mean, sendc, rsc, agc, mj,
    xsem, msem, s_sum, r_sum, s_cnt, r_cnt, s_mean, r_mean, s_rs, r_rs, s_ag, r_ag,
):
    comp, rows, cells = X.shape
    bins = modes.shape[0]
    nm = modes.shape[2]
    w = cells // tm
    blk = rows // space
    chunk = 256
    me_t = lax.axis_index("tm")
    me_s = lax.axis_index("space")

    xcopies = [pltpu.make_async_copy(snaps.at[c], X.at[c], xsem.at[c]) for c in range(comp)]
    for cp in xcopies:
        cp.start()
    for b in range(bins):
        pltpu.make_async_copy(modes.at[b], mo.at[:, pl.ds(b * nm, nm), :], msem.at[b]).start()

    barrier = pltpu.get_barrier_semaphore()
    for d in range(1, tm):
        pl.semaphore_signal(barrier, inc=1, device_id={"tm": lax.rem(me_t + d, tm)}, device_id_type=MESH)
    for d in range(1, space):
        pl.semaphore_signal(barrier, inc=1, device_id={"space": lax.rem(me_s + d, space)}, device_id_type=MESH)
    pl.semaphore_wait(barrier, tm - 1 + space - 1)

    hit = ownb[:, 0:1] == binrow[...]
    onehot = jnp.where(hit, 1.0, 0.0).astype(BF16)
    cnt[...] = jnp.broadcast_to(
        jnp.sum(jnp.where(hit, 1.0, 0.0), axis=1, keepdims=True), cnt.shape
    )
    for c in range(comp):
        xcopies[c].wait()
        for k in range(cells // 512):
            sl = pl.ds(k * 512, 512)
            sums[c, :, sl] = jnp.dot(onehot, X[c, :, sl], preferred_element_type=F32)

    def cols(q):
        return pl.ds(pl.multiple_of(q * w, w), w)

    sum_copies = []
    for d in range(1, tm):
        q = lax.rem(me_t + d, tm)
        a = pltpu.make_async_remote_copy(
            src_ref=sums.at[:, :, cols(q)], dst_ref=rsum.at[d - 1], send_sem=s_sum.at[d - 1],
            recv_sem=r_sum.at[d - 1], device_id={"tm": q}, device_id_type=MESH)
        e = pltpu.make_async_remote_copy(
            src_ref=cnt, dst_ref=rcnt.at[d - 1], send_sem=s_cnt.at[d - 1],
            recv_sem=r_cnt.at[d - 1], device_id={"tm": q}, device_id_type=MESH)
        a.start()
        e.start()
        sum_copies += [a, e]

    acc[...] = jnp.zeros_like(acc)

    def pair(p, _):
        for b in range(2):
            bb = 2 * p + b
            pltpu.make_async_copy(
                modes.at[bb], mo.at[:, pl.ds(pl.multiple_of(bb * nm, nm), nm), :], msem.at[bb]).wait()
        ms = pl.ds(pl.multiple_of(p * 2 * nm, 2 * nm), 2 * nm)

        def one(i, _):
            rs = pl.ds(pl.multiple_of(i * chunk, chunk), chunk)
            prod = lax.dot_general(X[0, rs, :], mo[0, ms, :], NT, preferred_element_type=F32)
            for c in range(1, comp):
                prod += lax.dot_general(X[c, rs, :], mo[c, ms, :], NT, preferred_element_type=F32)
            mine = binb[rs, :]
            acc[rs, :] += jnp.where(mine == 2 * p, prod[:, :nm], 0.0) + jnp.where(
                mine == 2 * p + 1, prod[:, nm:], 0.0)
            return 0

        lax.fori_loop(0, rows // chunk, one, 0)
        return 0

    half = bins // 4
    lax.fori_loop(0, half, pair, 0)

    for cp in sum_copies:
        cp.wait()
    total_cnt = cnt[...]
    for d in range(tm - 1):
        total_cnt = total_cnt + rcnt[d]
    mycols = cols(me_t)
    for c in range(comp):
        tot = sums[c, :, mycols]
        for d in range(tm - 1):
            tot = tot + rsum[d, c]
        mean[c, :, mycols] = (tot / total_cnt[:, 0:1]).astype(BF16)
    mean_copies = []
    for d in range(1, tm):
        a = pltpu.make_async_remote_copy(
            src_ref=mean.at[:, :, mycols], dst_ref=mean.at[:, :, mycols], send_sem=s_mean.at[d - 1],
            recv_sem=r_mean.at[d - 1], device_id={"tm": lax.rem(me_t + d, tm)}, device_id_type=MESH)
        a.start()
        mean_copies.append(a)

    lax.fori_loop(half, bins // 2, pair, 0)

    for d in range(1, tm):
        mean_copies[d - 1].wait_send()
        src = cols(lax.rem(me_t + tm - d, tm))
        pltpu.make_async_remote_copy(
            src_ref=mean.at[:, :, src], dst_ref=mean.at[:, :, src], send_sem=s_mean.at[d - 1],
            recv_sem=r_mean.at[d - 1], device_id={"tm": lax.rem(me_t + d, tm)}, device_id_type=MESH).wait_recv()
    mean_out[...] = mean[...]

    mj[...] = jnp.zeros_like(mj)

    def project(p, _):
        ms = pl.ds(pl.multiple_of(p * 2 * nm, 2 * nm), 2 * nm)
        prod = lax.dot_general(mean[0], mo[0, ms, :], NT, preferred_element_type=F32)
        for c in range(1, comp):
            prod += lax.dot_general(mean[c], mo[c, ms, :], NT, preferred_element_type=F32)
        own = ownb[...]
        mj[...] += jnp.where(own == 2 * p, prod[:, :nm], 0.0) + jnp.where(own == 2 * p + 1, prod[:, nm:], 0.0)
        return 0

    lax.fori_loop(0, bins // 2, project, 0)

    def block(s):
        return pl.ds(pl.multiple_of(s * blk, blk), blk)

    def corrected(s):
        rs = block(s)
        v = acc[rs, :]
        mine = binb[rs, :]
        for j in range(bins):
            v = v - jnp.where(mine == ownb[j:j + 1, :], mj[j:j + 1, :], 0.0)
        return v

    rs_copies = []
    for d in range(1, space):
        q = lax.rem(me_s + d, space)
        sendc[d - 1] = corrected(q).astype(BF16)
        a = pltpu.make_async_remote_copy(
            src_ref=sendc.at[d - 1], dst_ref=rsc.at[d - 1], send_sem=s_rs.at[d - 1],
            recv_sem=r_rs.at[d - 1], device_id={"space": q}, device_id_type=MESH)
        a.start()
        rs_copies.append(a)
    tot = corrected(me_s)
    for d in range(space - 1):
        rs_copies[d].wait()
        tot = tot + rsc[d].astype(F32)
    mine = block(me_s)
    agc[mine, :] = tot.astype(BF16)
    ag_copies = []
    for d in range(1, space):
        a = pltpu.make_async_remote_copy(
            src_ref=agc.at[mine], dst_ref=agc.at[mine], send_sem=s_ag.at[d - 1],
            recv_sem=r_ag.at[d - 1], device_id={"space": lax.rem(me_s + d, space)}, device_id_type=MESH)
        a.start()
        ag_copies.append(a)
    for d in range(1, space):
        ag_copies[d - 1].wait_send()
        src = block(lax.rem(me_s + space - d, space))
        pltpu.make_async_remote_copy(
            src_ref=agc.at[src], dst_ref=agc.at[src], send_sem=s_ag.at[d - 1],
            recv_sem=r_ag.at[d - 1], device_id={"space": lax.rem(me_s + d, space)}, device_id_type=MESH).wait_recv()
    coef_out[...] = agc[...]


def on_device(snaps, phase_bin, owner_order, modes):
    rows, comp, cells = snaps.shape
    bins, nm = modes.shape[0], modes.shape[1]
    tm, space = lax.axis_size("tm"), lax.axis_size("space")
    blk, w = rows // space, cells // tm
    binrow = phase_bin.reshape(1, rows)
    binb = jnp.broadcast_to(phase_bin[:, None], (rows, nm))
    ownb = jnp.broadcast_to(owner_order[:, None], (bins, nm))
    vm = pl.BlockSpec(memory_space=pltpu.VMEM)
    hbm = pl.BlockSpec(memory_space=pl.ANY)
    dma = pltpu.SemaphoreType.DMA
    coef, mean = pl.pallas_call(
        functools.partial(kernel, tm, space),
        out_shape=(
            jax.ShapeDtypeStruct((rows, nm), BF16),
            jax.ShapeDtypeStruct((comp, bins, cells), BF16),
        ),
        in_specs=[vm, vm, vm, hbm, hbm],
        out_specs=(vm, vm),
        scratch_shapes=[
            pltpu.VMEM((comp, rows, cells), BF16),
            pltpu.VMEM((comp, bins * nm, cells), BF16),
            pltpu.VMEM((rows, nm), F32),
            pltpu.VMEM((comp, bins, cells), F32),
            pltpu.VMEM((bins, 128), F32),
            pltpu.VMEM((tm - 1, comp, bins, w), F32),
            pltpu.VMEM((tm - 1, bins, 128), F32),
            pltpu.VMEM((comp, bins, cells), BF16),
            pltpu.VMEM((space - 1, blk, nm), BF16),
            pltpu.VMEM((space - 1, blk, nm), BF16),
            pltpu.VMEM((rows, nm), BF16),
            pltpu.VMEM((bins, nm), F32),
            dma((comp,)), dma((bins,)),
            dma((tm - 1,)), dma((tm - 1,)), dma((tm - 1,)), dma((tm - 1,)), dma((tm - 1,)), dma((tm - 1,)),
            dma((space - 1,)), dma((space - 1,)), dma((space - 1,)), dma((space - 1,)),
        ],
        compiler_params=pltpu.CompilerParams(
            collective_id=0, has_side_effects=True, vmem_limit_bytes=56 * 1024 * 1024
        ),
        cost_estimate=pl.CostEstimate(
            flops=2 * rows * bins * nm * comp * cells,
            bytes_accessed=2 * comp * cells * (rows + bins * nm), transcendentals=0),
    )(binrow, binb, ownb, snaps.transpose(1, 0, 2), modes.transpose(0, 2, 1, 3))
    own_rows = bins // tm
    own = lax.dynamic_slice_in_dim(mean, lax.axis_index("tm") * own_rows, own_rows, 1)
    return own.transpose(1, 0, 2), coef.astype(F32)


def solution(mesh):
    in_specs = (P("tm", None, "space"), P("tm"), P(), P(None, None, None, "space"))
    out_specs = (P("tm", None, "space"), P("tm", None))
    return jax.shard_map(
        on_device, mesh=mesh, in_specs=in_specs, out_specs=out_specs, check_vma=False
    )
```

time: 241 us -> 73.2 us (0.30)
  local copies, waits for them, and re-layouts: 125 us -> 4.55 us
  Pallas kernels: 0 us -> 66 us
  waiting for transfers between devices: 52.2 us -> 0 us
  matrix products: 26.7 us -> 0 us
  between operations: 14.2 us -> 0.64 us
  blocking collectives: 13.5 us -> 0 us
  other arithmetic: 6.89 us -> 1.78 us
    pallas_call x0 -> x1, Pallas kernels: none -> 66 us  [on_device(): pl.pallas_call(functools.partial(kernel, tm, space), out_shape=(jax.Shape...]
    psum x2 -> x0, waiting for transfers between devices: 52.2 us -> none  [the longest x1 52.2 us: on_device(): coefficients = lax.psum(picked, 'space')]
    gather x3 -> x0, local copies, waits for them, and re-layouts: 51.5 us -> none  [the longest x1 48 us: on_device(): gathered = jnp.take(flattened, source, axis=0, mode='fill', fill_value=0)]
    unnamed x7 -> x0, local copies, waits for them, and re-layouts: 51.2 us -> none
    dot_general x3 -> x0, matrix products: 26.7 us -> none  [the longest x1 17.7 us: on_device(): lax.dot_general(grouped, modes_flat, (((2,), (2,)), ((0,), (0,))), prefer...]
    reshape x1 -> x0, local copies, waits for them, and re-layouts: 16.7 us -> none  [on_device(): flattened = snaps.reshape(snap_rows, width)]
    psum x1 -> x0, blocking collectives: 13.5 us -> none  [on_device(): total_sums, total_counts = lax.psum((partial_sums, partial_counts), 'tm')]
    scatter x2 -> x0, local copies, waits for them, and re-layouts: 5.12 us -> none  [the longest x1 4.5 us: on_device(): jnp.full((bin_total * capacity,), snap_rows, jnp.int32).at[target]]
  transfers between devices with their start and end apart: 2 -> 0, of which waited for: 1 -> 0; matrix products, arithmetic and copies ran while one was open for 45% -> 0% of each run, Pallas kernels for 0% -> 0%
where the time goes in v1:
time: 73.2 us; the launch traced here: 72.9 us
  Pallas kernels  66 us (90%)
  local copies, waits for them, and re-layouts  4.55 us (6%)
  other arithmetic  1.78 us (2%)
    pallas_call x1, Pallas kernels, on_device(): pl.pallas_call(functools.partial(kernel, tm, space), out_shape=(jax.Shape...  66 us
    convert_element_type x1, other arithmetic, on_device(): return (own.transpose(1, 0, 2), coef.astype(F32))  1.78 us
    broadcast_in_dim x1, local copies, waits for them, and re-layouts, on_device(): binb = jnp.broadcast_to(phase_bin[:, None], (rows, nm))  1.68 us
    transpose x1, local copies, waits for them, and re-layouts, on_device(): return (own.transpose(1, 0, 2), coef.astype(F32))  1.54 us

profile of v1, /device:TPU:0, one launch (start us, length us, event | category | flops | bytes accessed | tf_op | source)
XLA Modules:
  0.0 72.9 jit_solution(4807988612820908574)
XLA Ops:
  0.6 1.7 %broadcast_in_dim.4.binb = s32[1024,128]{1,0:T(8,128)} broadcast(s32[1024]{0:T(1024)} %param.5), dimensions={0} | broadcast | bytes 528384 | tf_op jit(solution)/shard_map/broadcast_in_dim | solution.py:185
  2.3 1.3 %broadcast_in_dim.5.ownb = s32[16,128]{1,0:T(8,128)} broadcast(s32[16]{0:T(128)} %param.6), dimensions={0} | broadcast | bytes 8256 | tf_op jit(solution)/shard_map/broadcast_in_dim | solution.py:186
  3.6 66.0 %shard_map.59 = (bf16[1024,128]{1,0:T(8,128)(2,1)}, bf16[3,16,2048]{2,1,0:T(8,128)(2,1)}) custom-call(s32[1,1024]{1,0:T(1,128)} %bitcast.5, s32[1024,128]{1,0:T(8,128)} %broadcast_in_dim.4.binb, s32[16,128]{1,0:T(8,128)} %broadcast_in_dim.5.ownb, bf16[3,1024,2048]{2,1,0:T(8,128)(2,1)} %bitcast.7, bf16[16,3,128,2048]{3,2,1,0:T(8,128)(2,1)} %bitcast.6), custom_call_target="tpu_custom_call" | custom-call | flops 25769803776 | bytes 37748736 | tf_op jit(solution)/shard_map/pallas_call | solution.py:190
  69.6 1.5 %dynamic-slice_bitcast_fusion = bf16[4,3,2048]{2,0,1:T(4,128)(2,1)} fusion(bf16[3,16,2048]{2,1,0:T(8,128)(2,1)} %get-tuple-element.4, s32[]{:T(128)S(6)} %select_n.3), kind=kLoop, calls=%fused_computation | loop fusion | bytes 98308 | tf_op jit(solution)/shard_map/transpose | solution.py:224
  71.2 1.8 %convert_element_type.3 = f32[1024,128]{1,0:T(8,128)} convert(bf16[1024,128]{1,0:T(8,128)(2,1)} %get-tuple-element.5) | non-fusion elementwise | flops 131072 | bytes 786432 | tf_op jit(solution)/shard_map/convert_element_type | solution.py:224

commit v2 on v1

--- a/solution.py
+++ b/solution.py
@@ -14,8 +14,8 @@
 
 
 def kernel(
-    tm, space, binrow, binb, ownb, snaps, modes, coef_out, mean_out,
-    X, mo, acc, sums, cnt, rsum, rcnt, mean, sendc, rsc, agc, mj,
+    tm, space, binrow, ownrow, snaps, modes, coef_out, mean_out,
+    binb, ownb, X, mo, acc, sums, cnt, rsum, rcnt, mean, sendc, rsc, agc, mj,
     xsem, msem, s_sum, r_sum, s_cnt, r_cnt, s_mean, r_mean, s_rs, r_rs, s_ag, r_ag,
 ):
     comp, rows, cells = X.shape
@@ -23,15 +23,13 @@
     nm = modes.shape[2]
     w = cells // tm
     blk = rows // space
-    chunk = 256
+    chunk = 1024
     me_t = lax.axis_index("tm")
     me_s = lax.axis_index("space")
 
     xcopies = [pltpu.make_async_copy(snaps.at[c], X.at[c], xsem.at[c]) for c in range(comp)]
     for cp in xcopies:
         cp.start()
-    for b in range(bins):
-        pltpu.make_async_copy(modes.at[b], mo.at[:, pl.ds(b * nm, nm), :], msem.at[b]).start()
 
     barrier = pltpu.get_barrier_semaphore()
     for d in range(1, tm):
@@ -39,6 +37,17 @@
     for d in range(1, space):
         pl.semaphore_signal(barrier, inc=1, device_id={"space": lax.rem(me_s + d, space)}, device_id_type=MESH)
     pl.semaphore_wait(barrier, tm - 1 + space - 1)
+
+    for k in range(rows // nm):
+        sl = pl.ds(k * nm, nm)
+        binb[sl, :] = jnp.broadcast_to(binrow[:, sl], (nm, nm)).T
+    diagonal = lax.broadcasted_iota(jnp.int32, (bins, bins), 0) == lax.broadcasted_iota(
+        jnp.int32, (bins, bins), 1)
+    picked = jnp.where(diagonal, jnp.broadcast_to(ownrow[...].astype(F32), (bins, bins)), 0.0)
+    ownb[...] = jnp.broadcast_to(
+        jnp.sum(picked, axis=1, keepdims=True).astype(jnp.int32), ownb.shape)
+
+    fetch = [[], [0, 1], list(range(2, bins))]
 
     hit = ownb[:, 0:1] == binrow[...]
     onehot = jnp.where(hit, 1.0, 0.0).astype(BF16)
@@ -47,6 +56,8 @@
     )
     for c in range(comp):
         xcopies[c].wait()
+        for b in fetch[c]:
+            pltpu.make_async_copy(modes.at[b], mo.at[:, pl.ds(b * nm, nm), :], msem.at[b]).start()
         for k in range(cells // 512):
             sl = pl.ds(k * 512, 512)
             sums[c, :, sl] = jnp.dot(onehot, X[c, :, sl], preferred_element_type=F32)
@@ -182,8 +193,7 @@
     tm, space = lax.axis_size("tm"), lax.axis_size("space")
     blk, w = rows // space, cells // tm
     binrow = phase_bin.reshape(1, rows)
-    binb = jnp.broadcast_to(phase_bin[:, None], (rows, nm))
-    ownb = jnp.broadcast_to(owner_order[:, None], (bins, nm))
+    ownrow = owner_order.reshape(1, bins)
     vm = pl.BlockSpec(memory_space=pltpu.VMEM)
     hbm = pl.BlockSpec(memory_space=pl.ANY)
     dma = pltpu.SemaphoreType.DMA
@@ -193,9 +203,11 @@
             jax.ShapeDtypeStruct((rows, nm), BF16),
             jax.ShapeDtypeStruct((comp, bins, cells), BF16),
         ),
-        in_specs=[vm, vm, vm, hbm, hbm],
+        in_specs=[vm, vm, hbm, hbm],
         out_specs=(vm, vm),
         scratch_shapes=[
+            pltpu.VMEM((rows, nm), jnp.int32),
+            pltpu.VMEM((bins, nm), jnp.int32),
             pltpu.VMEM((comp, rows, cells), BF16),
             pltpu.VMEM((comp, bins * nm, cells), BF16),
             pltpu.VMEM((rows, nm), F32),
@@ -218,7 +230,7 @@
         cost_estimate=pl.CostEstimate(
             flops=2 * rows * bins * nm * comp * cells,
             bytes_accessed=2 * comp * cells * (rows + bins * nm), transcendentals=0),
-    )(binrow, binb, ownb, snaps.transpose(1, 0, 2), modes.transpose(0, 2, 1, 3))
+    )(binrow, ownrow, snaps.transpose(1, 0, 2), modes.transpose(0, 2, 1, 3))
     own_rows = bins // tm
     own = lax.dynamic_slice_in_dim(mean, lax.axis_index("tm") * own_rows, own_rows, 1)
     return own.transpose(1, 0, 2), coef.astype(F32)

time: 73.2 us -> 59.1 us (0.81)
  Pallas kernels: 66 us -> 55 us
  local copies, waits for them, and re-layouts: 4.55 us -> 1.55 us
    pallas_call x1, Pallas kernels: 66 us -> 55 us  [on_device(): pl.pallas_call(functools.partial(kernel, tm, space), out_shape=(jax.Shape...]
    broadcast_in_dim x2 -> x0, local copies, waits for them, and re-layouts: 3 us -> none  [the longest x1 1.68 us: on_device(): binb = jnp.broadcast_to(phase_bin[:, None], (rows, nm))]
where the time goes in v2:
time: 59.1 us; the launch traced here: 58.9 us
  Pallas kernels  55 us (93%)
  other arithmetic  1.78 us (3%)
  local copies, waits for them, and re-layouts  1.55 us (3%)
  between operations  0.64 us (1%)
    pallas_call x1, Pallas kernels, on_device(): pl.pallas_call(functools.partial(kernel, tm, space), out_shape=(jax.Shape...  55 us
    convert_element_type x1, other arithmetic, on_device(): return (own.transpose(1, 0, 2), coef.astype(F32))  1.78 us
    transpose x1, local copies, waits for them, and re-layouts, on_device(): return (own.transpose(1, 0, 2), coef.astype(F32))  1.55 us

profile of v2, /device:TPU:0, one launch (start us, length us, event | category | flops | bytes accessed | tf_op | source)
XLA Modules:
  0.0 58.9 jit_solution(8196787049377509016)
XLA Ops:
  0.6 55.0 %shard_map.59 = (bf16[1024,128]{1,0:T(8,128)(2,1)}, bf16[3,16,2048]{2,1,0:T(8,128)(2,1)}) custom-call(s32[1,1024]{1,0:T(1,128)} %bitcast.8, s32[1,16]{1,0:T(1,128)} %bitcast.9, bf16[3,1024,2048]{2,1,0:T(8,128)(2,1)} %bitcast.7, bf16[16,3,128,2048]{3,2,1,0:T(8,128)(2,1)} %bitcast.6), custom_call_target="tpu_custom_call" | custom-call | flops 25769803776 | bytes 37748736 | tf_op jit(solution)/shard_map/pallas_call | solution.py:200
  55.6 1.5 %dynamic-slice_bitcast_fusion = bf16[4,3,2048]{2,0,1:T(4,128)(2,1)} fusion(bf16[3,16,2048]{2,1,0:T(8,128)(2,1)} %get-tuple-element.4, s32[]{:T(128)S(6)} %select_n.3), kind=kLoop, calls=%fused_computation | loop fusion | bytes 98308 | tf_op jit(solution)/shard_map/transpose | solution.py:236
  57.2 1.8 %convert_element_type.3 = f32[1024,128]{1,0:T(8,128)} convert(bf16[1024,128]{1,0:T(8,128)(2,1)} %get-tuple-element.5) | non-fusion elementwise | flops 131072 | bytes 786432 | tf_op jit(solution)/shard_map/convert_element_type | solution.py:236

commit v3 on v2

--- a/solution.py
+++ b/solution.py
@@ -15,19 +15,19 @@
 
 def kernel(
     tm, space, binrow, ownrow, snaps, modes, coef_out, mean_out,
-    binb, ownb, X, mo, acc, sums, cnt, rsum, rcnt, mean, sendc, rsc, agc, mj,
+    binb, ownb, X, mo, acc, sums, cnt, rsum, rcnt, sendc, rsc, agc, mj,
     xsem, msem, s_sum, r_sum, s_cnt, r_cnt, s_mean, r_mean, s_rs, r_rs, s_ag, r_ag,
 ):
-    comp, rows, cells = X.shape
+    comp, rows, cells = snaps.shape
     bins = modes.shape[0]
     nm = modes.shape[2]
     w = cells // tm
     blk = rows // space
-    chunk = 1024
+    chunk = rows
     me_t = lax.axis_index("tm")
     me_s = lax.axis_index("space")
 
-    xcopies = [pltpu.make_async_copy(snaps.at[c], X.at[c], xsem.at[c]) for c in range(comp)]
+    xcopies = [pltpu.make_async_copy(snaps.at[c], X.at[c, pl.ds(0, rows), :], xsem.at[c]) for c in range(comp)]
     for cp in xcopies:
         cp.start()
 
@@ -60,7 +60,7 @@
             pltpu.make_async_copy(modes.at[b], mo.at[:, pl.ds(b * nm, nm), :], msem.at[b]).start()
         for k in range(cells // 512):
             sl = pl.ds(k * 512, 512)
-            sums[c, :, sl] = jnp.dot(onehot, X[c, :, sl], preferred_element_type=F32)
+            sums[c, :, sl] = jnp.dot(onehot, X[c, :rows, sl], preferred_element_type=F32)
 
     def cols(q):
         return pl.ds(pl.multiple_of(q * w, w), w)
@@ -113,37 +113,53 @@
         tot = sums[c, :, mycols]
         for d in range(tm - 1):
             tot = tot + rsum[d, c]
-        mean[c, :, mycols] = (tot / total_cnt[:, 0:1]).astype(BF16)
+        X[c, rows:, mycols] = (tot / total_cnt[:, 0:1]).astype(BF16)
     mean_copies = []
     for d in range(1, tm):
         a = pltpu.make_async_remote_copy(
-            src_ref=mean.at[:, :, mycols], dst_ref=mean.at[:, :, mycols], send_sem=s_mean.at[d - 1],
+            src_ref=X.at[:, pl.ds(rows, bins), mycols], dst_ref=X.at[:, pl.ds(rows, bins), mycols], send_sem=s_mean.at[d - 1],
             recv_sem=r_mean.at[d - 1], device_id={"tm": lax.rem(me_t + d, tm)}, device_id_type=MESH)
         a.start()
         mean_copies.append(a)
 
-    lax.fori_loop(half, bins // 2, pair, 0)
+    late = bins // 2 - 2
+    lax.fori_loop(half, late, pair, 0)
 
     for d in range(1, tm):
         mean_copies[d - 1].wait_send()
         src = cols(lax.rem(me_t + tm - d, tm))
         pltpu.make_async_remote_copy(
-            src_ref=mean.at[:, :, src], dst_ref=mean.at[:, :, src], send_sem=s_mean.at[d - 1],
+            src_ref=X.at[:, pl.ds(rows, bins), src], dst_ref=X.at[:, pl.ds(rows, bins), src], send_sem=s_mean.at[d - 1],
             recv_sem=r_mean.at[d - 1], device_id={"tm": lax.rem(me_t + d, tm)}, device_id_type=MESH).wait_recv()
-    mean_out[...] = mean[...]
+    mean_out[...] = X[:, rows:, :]
 
     mj[...] = jnp.zeros_like(mj)
 
     def project(p, _):
         ms = pl.ds(pl.multiple_of(p * 2 * nm, 2 * nm), 2 * nm)
-        prod = lax.dot_general(mean[0], mo[0, ms, :], NT, preferred_element_type=F32)
+        prod = lax.dot_general(X[0, rows:, :], mo[0, ms, :], NT, preferred_element_type=F32)
         for c in range(1, comp):
-            prod += lax.dot_general(mean[c], mo[c, ms, :], NT, preferred_element_type=F32)
+            prod += lax.dot_general(X[c, rows:, :], mo[c, ms, :], NT, preferred_element_type=F32)
         own = ownb[...]
         mj[...] += jnp.where(own == 2 * p, prod[:, :nm], 0.0) + jnp.where(own == 2 * p + 1, prod[:, nm:], 0.0)
         return 0
 
-    lax.fori_loop(0, bins // 2, project, 0)
+    def pair_and_mean(p, _):
+        for b in range(2):
+            bb = 2 * p + b
+            pltpu.make_async_copy(
+                modes.at[bb], mo.at[:, pl.ds(pl.multiple_of(bb * nm, nm), nm), :], msem.at[bb]).wait()
+        ms = pl.ds(pl.multiple_of(p * 2 * nm, 2 * nm), 2 * nm)
+        prod = lax.dot_general(X[0], mo[0, ms, :], NT, preferred_element_type=F32)
+        for c in range(1, comp):
+            prod += lax.dot_general(X[c], mo[c, ms, :], NT, preferred_element_type=F32)
+        for which, part, into in ((binb, prod[:rows], acc), (ownb, prod[rows:], mj)):
+            into[...] += jnp.where(which[...] == 2 * p, part[:, :nm], 0.0) + jnp.where(
+                which[...] == 2 * p + 1, part[:, nm:], 0.0)
+        return 0
+
+    lax.fori_loop(late, bins // 2, pair_and_mean, 0)
+    lax.fori_loop(0, late, project, 0)
 
     def block(s):
         return pl.ds(pl.multiple_of(s * blk, blk), blk)
@@ -208,14 +224,13 @@
         scratch_shapes=[
             pltpu.VMEM((rows, nm), jnp.int32),
             pltpu.VMEM((bins, nm), jnp.int32),
-            pltpu.VMEM((comp, rows, cells), BF16),
+            pltpu.VMEM((comp, rows + bins, cells), BF16),
             pltpu.VMEM((comp, bins * nm, cells), BF16),
             pltpu.VMEM((rows, nm), F32),
             pltpu.VMEM((comp, bins, cells), F32),
             pltpu.VMEM((bins, 128), F32),
             pltpu.VMEM((tm - 1, comp, bins, w), F32),
             pltpu.VMEM((tm - 1, bins, 128), F32),
-            pltpu.VMEM((comp, bins, cells), BF16),
             pltpu.VMEM((space - 1, blk, nm), BF16),
             pltpu.VMEM((space - 1, blk, nm), BF16),
             pltpu.VMEM((rows, nm), BF16),

time: 59.1 us -> 57.4 us (0.971)
  Pallas kernels: 55 us -> 53.3 us
    pallas_call x1, Pallas kernels: 55 us -> 53.3 us  [on_device(): pl.pallas_call(functools.partial(kernel, tm, space), out_shape=(jax.Shape...]
where the time goes in v3:
time: 57.4 us; the launch traced here: 57.2 us
  Pallas kernels  53.3 us (93%)
  other arithmetic  1.78 us (3%)
  local copies, waits for them, and re-layouts  1.55 us (3%)
  between operations  0.64 us (1%)
    pallas_call x1, Pallas kernels, on_device(): pl.pallas_call(functools.partial(kernel, tm, space), out_shape=(jax.Shape...  53.3 us
    convert_element_type x1, other arithmetic, on_device(): return (own.transpose(1, 0, 2), coef.astype(F32))  1.78 us
    transpose x1, local copies, waits for them, and re-layouts, on_device(): return (own.transpose(1, 0, 2), coef.astype(F32))  1.55 us

profile of v3, /device:TPU:0, one launch (start us, length us, event | category | flops | bytes accessed | tf_op | source)
XLA Modules:
  0.0 57.2 jit_solution(9355519600149473392)
XLA Ops:
  0.6 53.3 %shard_map.59 = (bf16[1024,128]{1,0:T(8,128)(2,1)}, bf16[3,16,2048]{2,1,0:T(8,128)(2,1)}) custom-call(s32[1,1024]{1,0:T(1,128)} %bitcast.8, s32[1,16]{1,0:T(1,128)} %bitcast.9, bf16[3,1024,2048]{2,1,0:T(8,128)(2,1)} %bitcast.7, bf16[16,3,128,2048]{3,2,1,0:T(8,128)(2,1)} %bitcast.6), custom_call_target="tpu_custom_call" | custom-call | flops 25769803776 | bytes 37748736 | tf_op jit(solution)/shard_map/pallas_call | solution.py:216
  53.9 1.5 %dynamic-slice_bitcast_fusion = bf16[4,3,2048]{2,0,1:T(4,128)(2,1)} fusion(bf16[3,16,2048]{2,1,0:T(8,128)(2,1)} %get-tuple-element.4, s32[]{:T(128)S(6)} %select_n.3), kind=kLoop, calls=%fused_computation | loop fusion | bytes 98308 | tf_op jit(solution)/shard_map/transpose | solution.py:251
  55.5 1.8 %convert_element_type.3 = f32[1024,128]{1,0:T(8,128)} convert(bf16[1024,128]{1,0:T(8,128)(2,1)} %get-tuple-element.5) | non-fusion elementwise | flops 131072 | bytes 786432 | tf_op jit(solution)/shard_map/convert_element_type | solution.py:251
